TPU v7x, 32 devices: a whole 2x2x4 slice. The times are simulated.
32 devices in a mesh: img: 16 (over z, y, x), lm: 2 (over core).
Axes of the slice: x: 2, y: 2, z: 4, core: 2. Of those that a mesh axis runs over, the one named last changes fastest.
Arguments:
- jac_point: float32 [6, 65536], P(None, ('img', 'lm')), may hold values from -4 to 4
- jac_cam: bfloat16 [65536, 256], P(('img', 'lm')), may hold values from -0.125 to 0.125
- resid: float32 [2, 65536], P(None, ('img', 'lm')), may hold values from -6 to 6
- point_ids: int32 [65536], P(('img', 'lm')), may hold values from 0 to 4095
- cam_ids: int32 [65536], P(('img', 'lm')), may hold values from 0 to 63
- owner_slot: int32 [64], replicated, may hold values from 0 to 63, each once
- damping: float32 [1], replicated, may hold values from 0.1 to 1
Outputs:
- landmark_step: float32 [3, 8192], P(None, 'lm')
- camera_gradient: float32 [64, 128], P(('img', 'lm'))
All inputs are finite; a program needn't handle non-finite values.
Results may differ from a plain program's by a relative error of at most 0.0029.
Values sent between devices are 32-bit elements; how exact they have to be, the bound alone decides.
A program may use at most 64 MiB of HBM per device.

v0:
```python
import jax
import jax.numpy as jnp
from jax import lax
from jax.sharding import PartitionSpec as P

CAMP = 128
BLOCK = 64
LM_BLOCKS = 64


def obs_terms(jac_point, resid):
    u0, u1, u2 = (jac_point[0], jac_point[1], jac_point[2])
    v0, v1, v2 = (jac_point[3], jac_point[4], jac_point[5])
    ru, rv = (resid[0], resid[1])
    return jnp.stack(
        [
            u0 * u0 + v0 * v0,
            u0 * u1 + v0 * v1,
            u0 * u2 + v0 * v2,
            u1 * u1 + v1 * v1,
            u1 * u2 + v1 * v2,
            u2 * u2 + v2 * v2,
            u0 * ru + v0 * rv,
            u1 * ru + v1 * rv,
            u2 * ru + v2 * rv,
        ],
        axis=1,
    )


def solve_points(stats, damping):
    factor = damping[0]
    h01, h02, h12 = (stats[1], stats[2], stats[4])
    a00 = stats[0] + factor * (stats[0] + 1.0)
    a11 = stats[3] + factor * (stats[3] + 1.0)
    a22 = stats[5] + factor * (stats[5] + 1.0)
    g0, g1, g2 = (stats[6], stats[7], stats[8])
    c00 = a11 * a22 - h12 * h12
    c01 = h02 * h12 - h01 * a22
    c02 = h01 * h12 - h02 * a11
    c11 = a00 * a22 - h02 * h02
    c12 = h01 * h02 - a00 * h12
    c22 = a00 * a11 - h01 * h01
    determ = a00 * c00 + h01 * c01 + h02 * c02
    s0 = -(c00 * g0 + c01 * g1 + c02 * g2) / determ
    s1 = -(c01 * g0 + c11 * g1 + c12 * g2) / determ
    s2 = -(c02 * g0 + c12 * g1 + c22 * g2) / determ
    return jnp.stack([s0, s1, s2], axis=0)


def per_device(jac_point, jac_cam, resid, point_ids, cam_ids, owner_slot, damping):
    slice_points = LM_BLOCKS * BLOCK
    terms = obs_terms(jac_point, resid)
    local_stats = jax.ops.segment_sum(terms, point_ids, num_segments=slice_points).T
    stats = lax.psum(local_stats, "img")
    step = solve_points(stats, damping)
    step_obs = jnp.take(step, point_ids, axis=1)
    cu = (
        resid[0]
        + jac_point[0] * step_obs[0]
        + jac_point[1] * step_obs[1]
        + jac_point[2] * step_obs[2]
    )
    cv = (
        resid[1]
        + jac_point[3] * step_obs[0]
        + jac_point[4] * step_obs[1]
        + jac_point[5] * step_obs[2]
    )
    cu_half = cu.astype(jnp.bfloat16)
    cv_half = cv.astype(jnp.bfloat16)
    slots = jnp.take(owner_slot, cam_ids)
    groups_all = owner_slot.shape[0]
    n_obs = cam_ids.shape[0]
    width = min(1024, n_obs)
    group_iota = jnp.arange(groups_all, dtype=jnp.int32)[:, None]
    partial_grad = jnp.zeros((groups_all, CAMP), jnp.float32)
    for block_index in range(n_obs // width):
        lo_row = block_index * width
        block_slots = slots[lo_row : lo_row + width]
        member = (block_slots[None, :] == group_iota).astype(jnp.bfloat16)
        left_u = member * cu_half[None, lo_row : lo_row + width]
        left_v = member * cv_half[None, lo_row : lo_row + width]
        cam_block = jac_cam[lo_row : lo_row + width]
        partial_grad = partial_grad + jnp.dot(
            left_u, cam_block[:, :CAMP], preferred_element_type=jnp.float32
        )
        partial_grad = partial_grad + jnp.dot(
            left_v, cam_block[:, CAMP:], preferred_element_type=jnp.float32
        )
    gradient = lax.psum_scatter(partial_grad, ("img", "lm"), scatter_dimension=0, tiled=True)
    return (step, gradient)


def solution(mesh):
    placed = (
        P(None, ("img", "lm")),
        P(("img", "lm"), None),
        P(None, ("img", "lm")),
        P(("img", "lm")),
        P(("img", "lm")),
        P(),
        P(),
    )
    return jax.shard_map(
        per_device,
        mesh=mesh,
        in_specs=placed,
        out_specs=(P(None, "lm"), P(("img", "lm"), None)),
        check_vma=False,
    )
```

profile of v0, /device:TPU:0, one launch (start us, length us, event | category | flops | bytes accessed | tf_op | source)
XLA Modules:
  0.0 193.5 jit_solution(9044518805957058838)
XLA Ops:
  7.2 0.0 all-reduce.3.cloned.1.call-start
  7.2 1.1 add_bitcast_fusion.5
  8.3 1.2 add_bitcast_fusion
  9.5 0.1 stack.4
  9.6 0.4 copy.119
  10.0 0.0 copy-start.4
  10.0 0.0 copy-start
  10.0 0.0 copy-start.5
  10.0 12.1 %scatter_custom_fusion = f32[4096,9]{1,0:T(8,128)S(1)} fusion(s32[2048]{0:T(1024)} %param.10, f32[2048,9]{1,0:T(8,128)S(1)} %copy.119, f32[]{:T(128)} %constant.30.clone.1), kind=kCustom, calls=%fused_computation.5 | custom fusion | flops 18432 | bytes 147968 | tf_op jit(solution)/shard_map/scatter-add | solution.py:54
  22.1 1.3 copy.120
  23.5 0.0 all-reduce.3.cloned.1.call-update
  23.5 0.0 copy-done.4
  23.5 0.0 copy-done
  23.5 0.7 fusion.33
  24.2 0.7 fusion.34
  25.0 0.7 fusion.35
  25.7 0.7 fusion.36
  27.0 0.0 copy-done.5
  27.0 0.0 copy-start.1
  27.0 0.0 copy-start.3
  27.0 39.7 %select_select_fusion = s32[2048]{0:T(1024)S(1)} fusion(s32[2048]{0:T(1024)S(1)} %copy-done.5, s32[]{:T(128)} %bitcast.11, s32[]{:T(128)} %bitcast.12, s32[]{:T(128)} %bitcast.13, s32[]{:T(128)} %bitcast.14, s32[]{:T(128)} %bitcast.15, s32[]{:T(128)} %bitcast.16, s32[]{:T(128)} %bitcast.17, s32[]{:T(128)} %bitcast.18, s32[]{:T(128)} %bitcast.19, ...), kind=kLoop, calls=%fused_computation.45 | loop fusion | flops 272384 | bytes 16640 | tf_op jit(solution)/shard_map/jit(_take)/select_n | solution.py:72
  66.8 66.3 %all-reduce.3.cloned.1.call-done = f32[9,4096]{1,0:T(8,128)} async-done(((f32[9,4096]{1,0:T(8,128)}), f32[9,4096]{1,0:T(8,128)}) %all-reduce.3.cloned.1.call-update) | async-done | bytes 147472 | tf_op jit(solution)/shard_map/psum | solution.py:55
  133.1 2.0 %negate_divide_fusion.2 = (f32[1,4096]{1,0:T(1,128)S(1)}, f32[1,4096]{1,0:T(1,128)S(1)}) fusion(f32[9,4096]{1,0:T(8,128)} %all-reduce.3.cloned.1.call-done, f32[]{:T(128)} %bitcast.86), kind=kLoop, calls=%fused_computation.39 | loop fusion | flops 122880 | bytes 180228 | tf_op jit(solution)/shard_map/div | solution.py:45
  135.1 2.0 %negate_divide_fusion.1 = (f32[1,4096]{1,0:T(1,128)S(1)}, f32[1,4096]{1,0:T(1,128)S(1)}) fusion(f32[1,4096]{1,0:T(1,128)S(1)} %get-tuple-element.13, f32[9,4096]{1,0:T(8,128)} %all-reduce.3.cloned.1.call-done, f32[]{:T(128)} %bitcast.87), kind=kLoop, calls=%fused_computation.35 | loop fusion | flops 155648 | bytes 196612 | tf_op jit(solution)/shard_map/div | solution.py:46
  137.2 0.0 copy-start.2
  137.2 0.6 copy.121
  137.9 5.5 %gather_fusion = f32[2048,3]{1,0:T(8,128)S(1)} fusion(f32[3,4096]{0,1:T(8,128)S(1)} %copy.121, s32[2048]{0:T(1024)S(1)} %fusion.27), kind=kCustom, calls=%fused_computation | custom fusion | bytes 57344 | tf_op jit(solution)/shard_map/jit(_take)/gather | solution.py:57
  143.3 0.0 copy-start.6
  143.4 0.3 copy.122
  143.7 0.0 copy-done.1
  143.7 0.0 copy-done.3
  143.7 0.1 add_convert_fusion
  143.8 0.1 slice_reduce_fusion
  143.9 1.1 fusion.7
  145.0 0.0 copy-done.2
  145.0 1.1 convolution_add_fusion.2
  146.1 0.0 copy-done.6
  146.2 0.2 convolution_add_fusion.1
  146.3 0.2 convolution_add_fusion
  146.5 39.5 %all-reduce = f32[64,128]{1,0:T(8,128)S(1)} all-reduce(f32[64,128]{1,0:T(8,128)S(1)} %convolution_add_fusion), channel_id=2, replica_groups=mesh['img'=16,'lm'=2] {'img','lm'}, use_global_device_ids=true, to_apply=%region_2.3.clone | all-reduce | flops 8192 | bytes 65536
  186.1 0.6 constant_dynamic-slice_fusion
  (5 shorter events, 0.1 us)
Async XLA Ops:
  7.2 126.0 %all-reduce.3.cloned.1.call-start = ((), (), s32[]{:S(2)}) async-start(), calls=%async_computation | async-start | bytes 524288 | tf_op jit(solution)/shard_map/psum | solution.py:55
  10.0 13.5 %copy-start.4 = (s32[2048]{0:T(1024)S(1)}, s32[2048]{0:T(1024)}, u32[]{:S(2)}) copy-start(s32[2048]{0:T(1024)} %param.10) | copy-start | bytes 24580
  10.0 13.5 %copy-start = (s32[64]{0:T(128)S(1)}, s32[64]{0:T(128)}, u32[]{:S(2)}) copy-start(s32[64]{0:T(128)} %param.12) | copy-start | bytes 772
  10.0 17.0 %copy-start.5 = (s32[2048]{0:T(1024)S(1)}, s32[2048]{0:T(1024)}, u32[]{:S(2)}) copy-start(s32[2048]{0:T(1024)} %param.11) | copy-start | bytes 24580
  27.0 116.7 %copy-start.1 = (f32[6,2048]{1,0:T(8,128)S(1)}, f32[6,2048]{1,0:T(8,128)}, u32[]{:S(2)}) copy-start(f32[6,2048]{1,0:T(8,128)} %param.7) | copy-start | bytes 147460
  27.0 116.7 %copy-start.3 = (f32[2,2048]{1,0:T(2,128)S(1)}, f32[2,2048]{1,0:T(2,128)}, u32[]{:S(2)}) copy-start(f32[2,2048]{1,0:T(2,128)} %param.9) | copy-start | bytes 49156
  137.2 7.8 %copy-start.2 = (f32[3,4096]{1,0:T(4,128)}, f32[3,4096]{1,0:T(4,128)S(1)}, u32[]{:S(2)}) copy-start(f32[3,4096]{1,0:T(4,128)S(1)} %pad_maximum_fusion) | copy-start | bytes 147460
  143.3 2.8 %copy-start.6 = (bf16[2048,256]{1,0:T(8,128)(2,1)S(1)}, bf16[2048,256]{1,0:T(8,128)(2,1)}, u32[]{:S(2)}) copy-start(bf16[2048,256]{1,0:T(8,128)(2,1)} %param.8) | copy-start | bytes 3145732
Sparse Core Ops, SparseCore 0:
  23.6 109.4 all-reduce.2
where the time goes:
time: 195 us; the launch traced here: 193 us
  waiting for transfers between devices  66.4 us (34%)
  other arithmetic  58.3 us (30%)
  blocking collectives  39.5 us (20%)
  between operations  14.9 us (8%)
  local copies, waits for them, and re-layouts  11.8 us (6%)
  matrix products  2.61 us (1%)
    psum x1, waiting for transfers between devices, per_device(): stats = lax.psum(local_stats, 'img')  66.3 us
    select_n x1, other arithmetic, per_device(): slots = jnp.take(owner_slot, cam_ids)  39.7 us
    unnamed x1, blocking collectives  39.5 us
    scatter-add x1, other arithmetic, per_device(): jax.ops.segment_sum(terms, point_ids, num_segments=slice_points)  12.1 us
    gather x2, local copies, waits for them, and re-layouts, per_device(): step_obs = jnp.take(step, point_ids, axis=1)  5.8 us
  transfers between devices with their start and end apart: 1, of which 1 were waited for; matrix products, arithmetic and copies ran while one was open for 22% of the time, Pallas kernels for 0%

commit v1 on v0

v1 whole, which is shorter than its diff:
```python
import functools
import jax
import jax.numpy as jnp
from jax import lax
from jax.experimental import pallas as pl
from jax.experimental.pallas import tpu as pltpu
from jax.sharding import PartitionSpec as P

CAMP = 128
BLOCK = 64
LM_BLOCKS = 64
LANES = 128
WIDE = 256
MESH = pl.DeviceIdType.MESH
F32 = jnp.float32
BF16 = jnp.bfloat16


def split_pair(x):
    high = x.astype(BF16).astype(F32)
    low = (x - high).astype(BF16).astype(F32)
    return high, low


def solve_points(stats, factor):
    h01, h02, h12 = (stats[1], stats[2], stats[4])
    a00 = stats[0] + factor * (stats[0] + 1.0)
    a11 = stats[3] + factor * (stats[3] + 1.0)
    a22 = stats[5] + factor * (stats[5] + 1.0)
    g0, g1, g2 = (stats[6], stats[7], stats[8])
    c00 = a11 * a22 - h12 * h12
    c01 = h02 * h12 - h01 * a22
    c02 = h01 * h12 - h02 * a11
    c11 = a00 * a22 - h02 * h02
    c12 = h01 * h02 - a00 * h12
    c22 = a00 * a11 - h01 * h01
    determ = a00 * c00 + h01 * c01 + h02 * c02
    s0 = -(c00 * g0 + c01 * g1 + c02 * g2) / determ
    s1 = -(c01 * g0 + c11 * g1 + c12 * g2) / determ
    s2 = -(c02 * g0 + c12 * g1 + c22 * g2) / determ
    return s0, s1, s2


def kernel(
    n_img, n_lm, n_own, groups,
    damping_ref, jac_ref, resid_ref, point_ref, cam_ref, slot_ref, jac_cam_ref,
    step_ref, grad_ref,
    cam_vmem, lo_hot, stat_send, stat_recv, table, part_send, part_recv,
    cam_sem, stat_send_sem, stat_recv_sem, extra_sem,
    step_send_sem, step_recv_sem, part_send_sem, part_recv_sem,
):
    n_dev = n_img * n_lm
    n_obs = point_ref.shape[1]
    rows = LM_BLOCKS * BLOCK // LANES
    n_hi = LM_BLOCKS * BLOCK // WIDE
    per_row = rows // n_own
    stride = n_img // n_own
    gpd = groups // n_dev
    img, lm = lax.axis_index("img"), lax.axis_index("lm")
    me = img * n_lm + lm
    own = img // stride if stride > 1 else img

    barrier = pltpu.get_barrier_semaphore()

    def greet(r, carry):
        peer = lax.rem(me + r, n_dev)
        pl.semaphore_signal(
            barrier, inc=1, device_id=(peer // n_lm, lax.rem(peer, n_lm)), device_id_type=MESH
        )
        return carry

    lax.fori_loop(1, n_dev, greet, 0)
    cam_copy = pltpu.make_async_copy(jac_cam_ref, cam_vmem, cam_sem)
    cam_copy.start()

    u = [jac_ref[a : a + 1, :] for a in range(3)]
    v = [jac_ref[3 + a : 4 + a, :] for a in range(3)]
    ru, rv = resid_ref[0:1, :], resid_ref[1:2, :]
    terms = [u[a] * u[b] + v[a] * v[b] for a, b in ((0, 0), (0, 1), (0, 2), (1, 1), (1, 2), (2, 2))]
    terms += [u[a] * ru + v[a] * rv for a in range(3)]
    point = point_ref[...]
    hi = point // WIDE
    lo = point - hi * WIDE
    hi_mask = lax.broadcasted_iota(jnp.int32, (n_hi, n_obs), 0) == hi
    lo_hot[...] = jnp.where(
        lax.broadcasted_iota(jnp.int32, (WIDE, n_obs), 0) == lo, 1.0, 0.0
    ).astype(BF16)
    blocks = []
    for part in zip(*[split_pair(t) for t in terms]):
        blocks += [jnp.where(hi_mask, t, 0.0).astype(BF16) for t in part]
    left = jnp.concatenate(blocks, axis=0)
    both = lax.dot_general(
        left, lo_hot[...], (((1,), (1,)), ((), ())), preferred_element_type=F32
    )
    local = both[: 9 * n_hi] + both[9 * n_hi :]
    for k in range(9):
        for half in range(WIDE // LANES):
            piece = local[k * n_hi : (k + 1) * n_hi, half * LANES : (half + 1) * LANES]
            if per_row == 2:
                stat_send[:, k, half, :] = piece
            else:
                for h in range(n_hi):
                    stat_send[h * (WIDE // LANES) + half, k] = piece[h : h + 1]

    pl.semaphore_wait(barrier, n_dev - 1)

    def send_stats(r, sem):
        owner = lax.rem(own + r, n_own)
        target = owner * stride
        return pltpu.make_async_remote_copy(
            src_ref=stat_send.at[owner],
            dst_ref=stat_recv.at[lax.rem(img - target + n_img - 1, n_img)],
            send_sem=sem,
            recv_sem=stat_recv_sem,
            device_id=(target, lm),
            device_id_type=MESH,
        )

    def stats_step(r, carry):
        send_stats(r, stat_send_sem).start()
        return carry

    lax.fori_loop(1, n_own, stats_step, 0)

    def step_copy(r):
        block = table.at[pl.ds(own * per_row, per_row)]
        return pltpu.make_async_remote_copy(
            src_ref=block,
            dst_ref=block,
            send_sem=step_send_sem,
            recv_sem=step_recv_sem,
            device_id=(lax.rem(img + r, n_img), lm),
            device_id_type=MESH,
        )

    def wait_for(ref, sem):
        pltpu.make_async_copy(ref, ref, sem).wait()

    def own_part():
        wait_for(stat_recv, stat_recv_sem)
        total = stat_send[own] + jnp.sum(stat_recv[...], axis=0)
        steps = solve_points([total[k] for k in range(9)], damping_ref[0])
        for half in range(per_row):
            for a in range(3):
                table[own * per_row + half, a : a + 1] = steps[a][half : half + 1]
            table[own * per_row + half, 3:4] = jnp.zeros((1, LANES), F32)

        def steps_out(r, carry):
            step_copy(r).start()
            return carry

        lax.fori_loop(1, n_img, steps_out, 0)

    row_slot = slot_ref[...]
    eye = lax.broadcasted_iota(jnp.int32, (groups, groups), 0) == lax.broadcasted_iota(
        jnp.int32, (groups, groups), 1
    )
    slot_column = jnp.sum(
        jnp.where(eye, row_slot.astype(F32), 0.0), axis=1, keepdims=True
    )
    group_iota = lax.broadcasted_iota(jnp.int32, (groups, n_obs), 0)
    slots = jnp.sum(
        jnp.where(group_iota == cam_ref[...], slot_column, 0.0), axis=0, keepdims=True
    ).astype(jnp.int32)

    if stride == 1:
        own_part()
        wait_for(table.at[pl.ds(0, rows - per_row)], step_recv_sem)
    else:
        is_owner = lax.rem(img, stride) == 0

        @pl.when(is_owner)
        def _():
            own_part()
            wait_for(table.at[pl.ds(0, rows - per_row)], step_recv_sem)

        @pl.when(jnp.logical_not(is_owner))
        def _():
            send_stats(0, extra_sem).start()
            wait_for(table, step_recv_sem)

    grid = table[...].reshape(n_hi, WIDE // LANES, 4, LANES)
    picked = [
        jnp.concatenate([grid[:, half, a, :] for half in range(WIDE // LANES)], axis=1)
        for a in range(3)
    ]
    pieces = []
    for part in zip(*[split_pair(t) for t in picked]):
        pieces += [t.astype(BF16) for t in part]
    found = jnp.dot(jnp.concatenate(pieces, axis=0), lo_hot[...], preferred_element_type=F32)
    step_obs = []
    for a in range(3):
        both_parts = found[a * n_hi : (a + 1) * n_hi] + found[(3 + a) * n_hi : (4 + a) * n_hi]
        step_obs.append(jnp.sum(jnp.where(hi_mask, both_parts, 0.0), axis=0, keepdims=True))
    cu = ru + u[0] * step_obs[0] + u[1] * step_obs[1] + u[2] * step_obs[2]
    cv = rv + v[0] * step_obs[0] + v[1] * step_obs[1] + v[2] * step_obs[2]
    member = group_iota == slots
    weights = jnp.concatenate(
        [jnp.where(member, cu, 0.0).astype(BF16), jnp.where(member, cv, 0.0).astype(BF16)], axis=0
    )
    cam_copy.wait()
    product = jnp.dot(weights, cam_vmem[...], preferred_element_type=F32)
    partial = product[:groups, :CAMP] + product[groups:, CAMP:]
    part_send[...] = partial.reshape(n_dev, gpd, CAMP)

    def part_step(r, carry):
        peer = lax.rem(me + r, n_dev)
        pltpu.make_async_remote_copy(
            src_ref=part_send.at[peer],
            dst_ref=part_recv.at[r - 1],
            send_sem=part_send_sem,
            recv_sem=part_recv_sem,
            device_id=(peer // n_lm, lax.rem(peer, n_lm)),
            device_id_type=MESH,
        ).start()
        return carry

    lax.fori_loop(1, n_dev, part_step, 0)

    for row in range(rows):
        step_ref[:, row * LANES : (row + 1) * LANES] = table[row, 0:3]

    wait_for(stat_send.at[pl.ds(0, n_own - 1)], stat_send_sem)
    if stride == 1:
        wait_for(table.at[pl.ds(0, rows - per_row)], step_send_sem)
    else:

        @pl.when(is_owner)
        def _():
            def one_step(r, carry):
                wait_for(table.at[pl.ds(0, per_row)], step_send_sem)
                return carry

            lax.fori_loop(1, n_img, one_step, 0)

        @pl.when(jnp.logical_not(is_owner))
        def _():
            wait_for(stat_send.at[0], extra_sem)

    wait_for(part_recv, part_recv_sem)
    grad_ref[...] = part_send[me] + jnp.sum(part_recv[...], axis=0)
    wait_for(part_send.at[pl.ds(0, n_dev - 1)], part_send_sem)


def solution(mesh):
    n_img, n_lm = mesh.shape["img"], mesh.shape["lm"]
    n_dev = n_img * n_lm
    points = LM_BLOCKS * BLOCK
    rows = points // LANES
    n_own = min(n_img, rows)
    per_row = rows // n_own

    def per_device(jac_point, jac_cam, resid, point_ids, cam_ids, owner_slot, damping):
        n_obs = cam_ids.shape[0]
        groups = owner_slot.shape[0]
        gpd = groups // n_dev
        vmem = pl.BlockSpec(memory_space=pltpu.VMEM)
        return pl.pallas_call(
            functools.partial(kernel, n_img, n_lm, n_own, groups),
            out_shape=(
                jax.ShapeDtypeStruct((3, points), F32),
                jax.ShapeDtypeStruct((gpd, CAMP), F32),
            ),
            in_specs=[pl.BlockSpec(memory_space=pltpu.SMEM)]
            + [vmem] * 5
            + [pl.BlockSpec(memory_space=pl.ANY)],
            out_specs=(vmem, vmem),
            scratch_shapes=[
                pltpu.VMEM((n_obs, 2 * CAMP), BF16),
                pltpu.VMEM((WIDE, n_obs), BF16),
                pltpu.VMEM((n_own, 9, per_row, LANES), F32),
                pltpu.VMEM((n_img - 1, 9, per_row, LANES), F32),
                pltpu.VMEM((rows, 4, LANES), F32),
                pltpu.VMEM((n_dev, gpd, CAMP), F32),
                pltpu.VMEM((n_dev - 1, gpd, CAMP), F32),
            ]
            + [pltpu.SemaphoreType.DMA] * 8,
            compiler_params=pltpu.CompilerParams(
                collective_id=0,
                has_side_effects=True,
                vmem_limit_bytes=(24 if groups <= 256 else 56) * 2**20,
            ),
        )(
            damping,
            jac_point,
            resid,
            point_ids.reshape(1, n_obs),
            cam_ids.reshape(1, n_obs),
            owner_slot.reshape(1, groups),
            jac_cam,
        )

    placed = (
        P(None, ("img", "lm")),
        P(("img", "lm"), None),
        P(None, ("img", "lm")),
        P(("img", "lm")),
        P(("img", "lm")),
        P(),
        P(),
    )
    return jax.shard_map(
        per_device,
        mesh=mesh,
        in_specs=placed,
        out_specs=(P(None, "lm"), P(("img", "lm"), None)),
        check_vma=False,
    )
```

time: 195 us -> 29.2 us (0.15)
  waiting for transfers between devices: 66.4 us -> 0 us
  other arithmetic: 58.3 us -> 0 us
  blocking collectives: 39.5 us -> 0 us
  Pallas kernels: 0 us -> 21.5 us
  between operations: 14.9 us -> 1.3 us
  local copies, waits for them, and re-layouts: 11.8 us -> 6.01 us
  matrix products: 2.61 us -> 0 us
    psum x1 -> x0, waiting for transfers between devices: 66.3 us -> none  [per_device(): stats = lax.psum(local_stats, 'img')]
    select_n x2 -> x0, other arithmetic: 39.7 us -> none  [the longest x1 39.7 us: per_device(): slots = jnp.take(owner_slot, cam_ids)]
    unnamed x1 -> x0, blocking collectives: 39.5 us -> none
    pallas_call x0 -> x1, Pallas kernels: none -> 21.5 us  [per_device(): pl.pallas_call(functools.partial(kernel, n_img, n_lm, n_own, groups), out...]
    scatter-add x1 -> x0, other arithmetic: 12.1 us -> none  [per_device(): jax.ops.segment_sum(terms, point_ids, num_segments=slice_points)]
    gather x6 -> x0, local copies, waits for them, and re-layouts: 8.64 us -> none  [the longest x2 5.8 us: per_device(): step_obs = jnp.take(step, point_ids, axis=1)]
    unnamed x15 -> x14, local copies, waits for them, and re-layouts: 0.62 us -> 6.01 us
    div x2 -> x0, other arithmetic: 4.02 us -> none  [the longest x1 2.03 us: solve_points(): s1 = -(c01 * g0 + c11 * g1 + c12 * g2) / determ]
  transfers between devices with their start and end apart: 1 -> 0, of which waited for: 1 -> 0; matrix products, arithmetic and copies ran while one was open for 22% -> 0% of each run, Pallas kernels for 0% -> 0%
where the time goes in v1:
time: 29.2 us; the launch traced here: 28.8 us
  Pallas kernels  21.5 us (74%)
  local copies, waits for them, and re-layouts  6.01 us (21%)
  between operations  1.3 us (4%)
    pallas_call x1, Pallas kernels, per_device(): pl.pallas_call(functools.partial(kernel, n_img, n_lm, n_own, groups), out...  21.5 us
    unnamed x14, local copies, waits for them, and re-layouts  6.01 us

profile of v1, /device:TPU:0, one launch (start us, length us, event | category | flops | bytes accessed | tf_op | source)
XLA Modules:
  0.0 28.8 jit_solution(6579828285013389031)
XLA Ops:
  1.3 0.0 copy-start.5
  1.3 0.6 %copy-done.5 = s32[64]{0:T(128)S(1)} copy-done((s32[64]{0:T(128)S(1)}, s32[64]{0:T(128)}, u32[]{:S(2)}) %copy-start.5) | copy-done | bytes 280
  1.9 0.0 copy-start
  1.9 1.2 %copy-done = bf16[2048,256]{1,0:T(8,128)(2,1)S(1)} copy-done((bf16[2048,256]{1,0:T(8,128)(2,1)S(1)}, bf16[2048,256]{1,0:T(8,128)(2,1)}, u32[]{:S(2)}) %copy-start) | copy-done | bytes 1048600
  3.2 0.0 copy-start.1
  3.2 0.8 %copy-done.1 = f32[6,2048]{1,0:T(8,128)S(1)} copy-done((f32[6,2048]{1,0:T(8,128)S(1)}, f32[6,2048]{1,0:T(8,128)}, u32[]{:S(2)}) %copy-start.1) | copy-done | bytes 49176
  4.0 0.0 copy-start.2
  4.0 0.7 %copy-done.2 = f32[2,2048]{1,0:T(2,128)S(1)} copy-done((f32[2,2048]{1,0:T(2,128)S(1)}, f32[2,2048]{1,0:T(2,128)}, u32[]{:S(2)}) %copy-start.2) | copy-done | bytes 16408
  4.7 0.0 copy-start.3
  4.7 0.7 %copy-done.3 = s32[2048]{0:T(1024)S(1)} copy-done((s32[2048]{0:T(1024)S(1)}, s32[2048]{0:T(1024)}, u32[]{:S(2)}) %copy-start.3) | copy-done | bytes 8216
  5.4 0.0 copy-start.4
  5.4 0.7 %copy-done.4 = s32[2048]{0:T(1024)S(1)} copy-done((s32[2048]{0:T(1024)S(1)}, s32[2048]{0:T(1024)}, u32[]{:S(2)}) %copy-start.4) | copy-done | bytes 8216
  6.1 21.5 %shard_map.86 = (f32[3,4096]{1,0:T(4,128)S(1)}, f32[2,128]{1,0:T(2,128)S(1)}) custom-call(f32[1]{0:T(128)S(6)} %copy.11.damping_ref, f32[6,2048]{1,0:T(8,128)S(1)} %copy-done.1, f32[2,2048]{1,0:T(2,128)S(1)} %copy-done.2, s32[1,2048]{1,0:T(1,128)S(1)} %bitcast.3, s32[1,2048]{1,0:T(1,128)S(1)} %bitcast.4, s32[1,64]{1,0:T(1,128)S(1)} %bitcast.5, ...), custom_call_target="tpu_custom_call" | custom-call | tf_op jit(solution)/shard_map/pallas_call | solution.py:258
  27.6 0.6 %copy.12 = f32[3,4096]{1,0:T(4,128)} copy(f32[3,4096]{1,0:T(4,128)S(1)} %get-tuple-element.4) | data formatting | bytes 98304
  28.3 0.6 %copy.13 = f32[2,128]{1,0:T(2,128)} copy(f32[2,128]{1,0:T(2,128)S(1)} %get-tuple-element.5) | data formatting | bytes 2048
Async XLA Ops:
  1.3 0.7 %copy-start.5 = (s32[64]{0:T(128)S(1)}, s32[64]{0:T(128)}, u32[]{:S(2)}) copy-start(s32[64]{0:T(128)} %param.12) | copy-start | bytes 772
  1.9 1.2 %copy-start = (bf16[2048,256]{1,0:T(8,128)(2,1)S(1)}, bf16[2048,256]{1,0:T(8,128)(2,1)}, u32[]{:S(2)}) copy-start(bf16[2048,256]{1,0:T(8,128)(2,1)} %jac_cam_ref.1) | copy-start | bytes 3145732
  3.2 0.8 %copy-start.1 = (f32[6,2048]{1,0:T(8,128)S(1)}, f32[6,2048]{1,0:T(8,128)}, u32[]{:S(2)}) copy-start(f32[6,2048]{1,0:T(8,128)} %jac_ref.1) | copy-start | bytes 147460
  4.0 0.7 %copy-start.2 = (f32[2,2048]{1,0:T(2,128)S(1)}, f32[2,2048]{1,0:T(2,128)}, u32[]{:S(2)}) copy-start(f32[2,2048]{1,0:T(2,128)} %resid_ref.1) | copy-start | bytes 49156
  4.7 0.7 %copy-start.3 = (s32[2048]{0:T(1024)S(1)}, s32[2048]{0:T(1024)}, u32[]{:S(2)}) copy-start(s32[2048]{0:T(1024)} %param.10) | copy-start | bytes 24580
  5.4 0.7 %copy-start.4 = (s32[2048]{0:T(1024)S(1)}, s32[2048]{0:T(1024)}, u32[]{:S(2)}) copy-start(s32[2048]{0:T(1024)} %param.11) | copy-start | bytes 24580

commit v2 on v1

--- a/solution.py
+++ b/solution.py
@@ -10,6 +10,7 @@
 BLOCK = 64
 LM_BLOCKS = 64
 LANES = 128
+VMEM_BYTES = 2**26 - 2**18
 WIDE = 256
 MESH = pl.DeviceIdType.MESH
 F32 = jnp.float32
@@ -43,10 +44,10 @@
 
 def kernel(
     n_img, n_lm, n_own, groups,
-    damping_ref, jac_ref, resid_ref, point_ref, cam_ref, slot_ref, jac_cam_ref,
-    step_ref, grad_ref,
-    cam_vmem, lo_hot, stat_send, stat_recv, table, part_send, part_recv,
-    cam_sem, stat_send_sem, stat_recv_sem, extra_sem,
+    damping_ref, jac_hbm, resid_hbm, point_hbm, cam_hbm, slot_hbm, jac_cam_hbm,
+    step_hbm, grad_hbm,
+    step_ref, grad_ref, jac_ref, resid_ref, point_ref, cam_ref, slot_ref, cam_vmem, lo_hot, stat_send, stat_recv, table, part_send, part_recv,
+    in_sems, out_sems, stat_send_sem, stat_recv_sem, extra_sem,
     step_send_sem, step_recv_sem, part_send_sem, part_recv_sem,
 ):
     n_dev = n_img * n_lm
@@ -60,24 +61,49 @@
     me = img * n_lm + lm
     own = img // stride if stride > 1 else img
 
+    copies = [
+        pltpu.make_async_copy(source, target, in_sems.at[i])
+        for i, (source, target) in enumerate(
+            [
+                (point_hbm, point_ref),
+                (jac_hbm, jac_ref),
+                (resid_hbm, resid_ref),
+                (cam_hbm, cam_ref),
+                (slot_hbm, slot_ref),
+                (jac_cam_hbm, cam_vmem),
+            ]
+        )
+    ]
+    for copy in copies:
+        copy.start()
+
+    def wrap(index, extent):
+        return jnp.where(index >= extent, index - extent, index)
+
+    def repeat(first, last, body):
+        if last <= 64:
+            for r in range(first, last):
+                body(r)
+        else:
+            lax.fori_loop(first, last, lambda r, carry: (body(r), carry)[1], 0)
+
+    def every_peer(body):
+        for d_lm in range(n_lm):
+            peer_lm = wrap(lm + d_lm, n_lm)
+
+            def one(d_img, d_lm=d_lm, peer_lm=peer_lm):
+                body(wrap(img + d_img, n_img), peer_lm, d_img * n_lm + d_lm - 1)
+
+            repeat(1 if d_lm == 0 else 0, n_img, one)
+
     barrier = pltpu.get_barrier_semaphore()
-
-    def greet(r, carry):
-        peer = lax.rem(me + r, n_dev)
-        pl.semaphore_signal(
-            barrier, inc=1, device_id=(peer // n_lm, lax.rem(peer, n_lm)), device_id_type=MESH
-        )
-        return carry
-
-    lax.fori_loop(1, n_dev, greet, 0)
-    cam_copy = pltpu.make_async_copy(jac_cam_ref, cam_vmem, cam_sem)
-    cam_copy.start()
-
-    u = [jac_ref[a : a + 1, :] for a in range(3)]
-    v = [jac_ref[3 + a : 4 + a, :] for a in range(3)]
-    ru, rv = resid_ref[0:1, :], resid_ref[1:2, :]
-    terms = [u[a] * u[b] + v[a] * v[b] for a, b in ((0, 0), (0, 1), (0, 2), (1, 1), (1, 2), (2, 2))]
-    terms += [u[a] * ru + v[a] * rv for a in range(3)]
+    every_peer(
+        lambda peer_img, peer_lm, r: pl.semaphore_signal(
+            barrier, inc=1, device_id=(peer_img, peer_lm), device_id_type=MESH
+        )
+    )
+
+    copies[0].wait()
     point = point_ref[...]
     hi = point // WIDE
     lo = point - hi * WIDE
@@ -85,6 +111,13 @@
     lo_hot[...] = jnp.where(
         lax.broadcasted_iota(jnp.int32, (WIDE, n_obs), 0) == lo, 1.0, 0.0
     ).astype(BF16)
+    copies[1].wait()
+    copies[2].wait()
+    u = [jac_ref[a : a + 1, :] for a in range(3)]
+    v = [jac_ref[3 + a : 4 + a, :] for a in range(3)]
+    ru, rv = resid_ref[0:1, :], resid_ref[1:2, :]
+    terms = [u[a] * u[b] + v[a] * v[b] for a, b in ((0, 0), (0, 1), (0, 2), (1, 1), (1, 2), (2, 2))]
+    terms += [u[a] * ru + v[a] * rv for a in range(3)]
     blocks = []
     for part in zip(*[split_pair(t) for t in terms]):
         blocks += [jnp.where(hi_mask, t, 0.0).astype(BF16) for t in part]
@@ -105,22 +138,18 @@
     pl.semaphore_wait(barrier, n_dev - 1)
 
     def send_stats(r, sem):
-        owner = lax.rem(own + r, n_own)
+        owner = wrap(own + r, n_own)
         target = owner * stride
         return pltpu.make_async_remote_copy(
             src_ref=stat_send.at[owner],
-            dst_ref=stat_recv.at[lax.rem(img - target + n_img - 1, n_img)],
+            dst_ref=stat_recv.at[wrap(img - target + n_img - 1, n_img)],
             send_sem=sem,
             recv_sem=stat_recv_sem,
             device_id=(target, lm),
             device_id_type=MESH,
         )
 
-    def stats_step(r, carry):
-        send_stats(r, stat_send_sem).start()
-        return carry
-
-    lax.fori_loop(1, n_own, stats_step, 0)
+    repeat(1, n_own, lambda r: send_stats(r, stat_send_sem).start())
 
     def step_copy(r):
         block = table.at[pl.ds(own * per_row, per_row)]
@@ -129,7 +158,7 @@
             dst_ref=block,
             send_sem=step_send_sem,
             recv_sem=step_recv_sem,
-            device_id=(lax.rem(img + r, n_img), lm),
+            device_id=(wrap(img + r, n_img), lm),
             device_id_type=MESH,
         )
 
@@ -144,13 +173,10 @@
             for a in range(3):
                 table[own * per_row + half, a : a + 1] = steps[a][half : half + 1]
             table[own * per_row + half, 3:4] = jnp.zeros((1, LANES), F32)
-
-        def steps_out(r, carry):
-            step_copy(r).start()
-            return carry
-
-        lax.fori_loop(1, n_img, steps_out, 0)
-
+        repeat(1, n_img, lambda r: step_copy(r).start())
+
+    copies[3].wait()
+    copies[4].wait()
     row_slot = slot_ref[...]
     eye = lax.broadcasted_iota(jnp.int32, (groups, groups), 0) == lax.broadcasted_iota(
         jnp.int32, (groups, groups), 1
@@ -198,27 +224,26 @@
     weights = jnp.concatenate(
         [jnp.where(member, cu, 0.0).astype(BF16), jnp.where(member, cv, 0.0).astype(BF16)], axis=0
     )
-    cam_copy.wait()
+    copies[5].wait()
     product = jnp.dot(weights, cam_vmem[...], preferred_element_type=F32)
     partial = product[:groups, :CAMP] + product[groups:, CAMP:]
     part_send[...] = partial.reshape(n_dev, gpd, CAMP)
 
-    def part_step(r, carry):
-        peer = lax.rem(me + r, n_dev)
-        pltpu.make_async_remote_copy(
-            src_ref=part_send.at[peer],
-            dst_ref=part_recv.at[r - 1],
+    every_peer(
+        lambda peer_img, peer_lm, r: pltpu.make_async_remote_copy(
+            src_ref=part_send.at[peer_img * n_lm + peer_lm],
+            dst_ref=part_recv.at[r],
             send_sem=part_send_sem,
             recv_sem=part_recv_sem,
-            device_id=(peer // n_lm, lax.rem(peer, n_lm)),
+            device_id=(peer_img, peer_lm),
             device_id_type=MESH,
         ).start()
-        return carry
-
-    lax.fori_loop(1, n_dev, part_step, 0)
+    )
 
     for row in range(rows):
         step_ref[:, row * LANES : (row + 1) * LANES] = table[row, 0:3]
+    step_out = pltpu.make_async_copy(step_ref, step_hbm, out_sems.at[0])
+    step_out.start()
 
     wait_for(stat_send.at[pl.ds(0, n_own - 1)], stat_send_sem)
     if stride == 1:
@@ -239,7 +264,22 @@
 
     wait_for(part_recv, part_recv_sem)
     grad_ref[...] = part_send[me] + jnp.sum(part_recv[...], axis=0)
+    grad_out = pltpu.make_async_copy(grad_ref, grad_hbm, out_sems.at[1])
+    grad_out.start()
     wait_for(part_send.at[pl.ds(0, n_dev - 1)], part_send_sem)
+    step_out.wait()
+    grad_out.wait()
+
+
+def write_out(step_in, grad_in, step_hbm, grad_hbm, sems):
+    copies = [
+        pltpu.make_async_copy(step_in, step_hbm, sems.at[0]),
+        pltpu.make_async_copy(grad_in, grad_hbm, sems.at[1]),
+    ]
+    for copy in copies:
+        copy.start()
+    for copy in copies:
+        copy.wait()
 
 
 def solution(mesh):
@@ -254,18 +294,25 @@
         n_obs = cam_ids.shape[0]
         groups = owner_slot.shape[0]
         gpd = groups // n_dev
-        vmem = pl.BlockSpec(memory_space=pltpu.VMEM)
-        return pl.pallas_call(
+        hbm = pl.BlockSpec(memory_space=pltpu.HBM)
+        shapes = (
+            jax.ShapeDtypeStruct((3, points), F32),
+            jax.ShapeDtypeStruct((gpd, CAMP), F32),
+        )
+        results = pl.pallas_call(
             functools.partial(kernel, n_img, n_lm, n_own, groups),
-            out_shape=(
-                jax.ShapeDtypeStruct((3, points), F32),
-                jax.ShapeDtypeStruct((gpd, CAMP), F32),
-            ),
+            out_shape=shapes,
             in_specs=[pl.BlockSpec(memory_space=pltpu.SMEM)]
-            + [vmem] * 5
-            + [pl.BlockSpec(memory_space=pl.ANY)],
-            out_specs=(vmem, vmem),
+            + [hbm] * 6,
+            out_specs=(hbm, hbm),
             scratch_shapes=[
+                pltpu.VMEM((3, points), F32),
+                pltpu.VMEM((gpd, CAMP), F32),
+                pltpu.VMEM(jac_point.shape, F32),
+                pltpu.VMEM(resid.shape, F32),
+                pltpu.VMEM((1, n_obs), jnp.int32),
+                pltpu.VMEM((1, n_obs), jnp.int32),
+                pltpu.VMEM((1, groups), jnp.int32),
                 pltpu.VMEM((n_obs, 2 * CAMP), BF16),
                 pltpu.VMEM((WIDE, n_obs), BF16),
                 pltpu.VMEM((n_own, 9, per_row, LANES), F32),
@@ -274,11 +321,12 @@
                 pltpu.VMEM((n_dev, gpd, CAMP), F32),
                 pltpu.VMEM((n_dev - 1, gpd, CAMP), F32),
             ]
-            + [pltpu.SemaphoreType.DMA] * 8,
+            + [pltpu.SemaphoreType.DMA((6,)), pltpu.SemaphoreType.DMA((2,))]
+            + [pltpu.SemaphoreType.DMA] * 7,
             compiler_params=pltpu.CompilerParams(
                 collective_id=0,
                 has_side_effects=True,
-                vmem_limit_bytes=(24 if groups <= 256 else 56) * 2**20,
+                vmem_limit_bytes=VMEM_BYTES,
             ),
         )(
             damping,
@@ -289,6 +337,14 @@
             owner_slot.reshape(1, groups),
             jac_cam,
         )
+        return pl.pallas_call(
+            write_out,
+            out_shape=shapes,
+            in_specs=[hbm, hbm],
+            out_specs=(hbm, hbm),
+            scratch_shapes=[pltpu.SemaphoreType.DMA((2,))],
+            compiler_params=pltpu.CompilerParams(vmem_limit_bytes=VMEM_BYTES),
+        )(*results)
 
     placed = (
         P(None, ("img", "lm")),

time: 29.2 us -> 26.6 us (0.911)
  local copies, waits for them, and re-layouts: 6.01 us -> 0 us
  Pallas kernels: 21.5 us -> 25.1 us
    unnamed x14 -> x0, local copies, waits for them, and re-layouts: 6.01 us -> none
    pallas_call x0 -> x1, Pallas kernels: none -> 3.14 us  [per_device(): pl.pallas_call(write_out, out_shape=shapes, in_specs=[hbm, hbm], out_spec...]
    pallas_call x1, Pallas kernels: 21.5 us -> 22 us  [per_device(): pl.pallas_call(functools.partial(kernel, n_img, n_lm, n_own, groups), out...]
where the time goes in v2:
time: 26.6 us; the launch traced here: 26.4 us
  Pallas kernels  25.1 us (94%)
  between operations  1.29 us (5%)
    pallas_call x1, Pallas kernels, per_device(): pl.pallas_call(functools.partial(kernel, n_img, n_lm, n_own, groups), out...  22 us
    pallas_call x1, Pallas kernels, per_device(): pl.pallas_call(write_out, out_shape=shapes, in_specs=[hbm, hbm], out_spec...  3.14 us

profile of v2, /device:TPU:0, one launch (start us, length us, event | category | flops | bytes accessed | tf_op | source)
XLA Modules:
  0.0 26.4 jit_solution(15359873968967131309)
XLA Ops:
  1.3 22.0 %shard_map.86 = (f32[3,4096]{1,0:T(4,128)}, f32[2,128]{1,0:T(2,128)}) custom-call(f32[1]{0:T(128)S(6)} %copy.9.damping_ref, f32[6,2048]{1,0:T(8,128)} %jac_hbm.1, f32[2,2048]{1,0:T(2,128)} %resid_hbm.1, s32[1,2048]{1,0:T(1,128)} %bitcast.3, s32[1,2048]{1,0:T(1,128)} %bitcast.4, s32[1,64]{1,0:T(1,128)} %bitcast.5, bf16[2048,256]{1,0:T(8,128)(2,1)} %jac_cam_hbm.1), custom_call_target="tpu_custom_call" | custom-call | tf_op jit(solution)/shard_map/pallas_call | solution.py:302
  23.2 3.1 %shard_map.87 = (f32[3,4096]{1,0:T(4,128)}, f32[2,128]{1,0:T(2,128)}) custom-call(f32[3,4096]{1,0:T(4,128)} %get-tuple-element.4.step_in, f32[2,128]{1,0:T(2,128)} %get-tuple-element.5.grad_in), custom_call_target="tpu_custom_call" | custom-call | tf_op jit(solution)/shard_map/pallas_call | solution.py:340

commit v3 on v2

--- a/solution.py
+++ b/solution.py
@@ -12,6 +12,7 @@
 LANES = 128
 VMEM_BYTES = 2**26 - 2**18
 WIDE = 256
+CHUNK = 512
 MESH = pl.DeviceIdType.MESH
 F32 = jnp.float32
 BF16 = jnp.bfloat16
@@ -46,7 +47,7 @@
     n_img, n_lm, n_own, groups,
     damping_ref, jac_hbm, resid_hbm, point_hbm, cam_hbm, slot_hbm, jac_cam_hbm,
     step_hbm, grad_hbm,
-    step_ref, grad_ref, jac_ref, resid_ref, point_ref, cam_ref, slot_ref, cam_vmem, lo_hot, stat_send, stat_recv, table, part_send, part_recv,
+    step_ref, grad_ref, jac_ref, resid_ref, point_ref, cam_ref, slot_ref, slot_row, cam_vmem, lo_hot, stat_send, stat_recv, table, part_send, part_recv,
     in_sems, out_sems, stat_send_sem, stat_recv_sem, extra_sem,
     step_send_sem, step_recv_sem, part_send_sem, part_recv_sem,
 ):
@@ -103,29 +104,34 @@
         )
     )
 
-    copies[0].wait()
-    point = point_ref[...]
-    hi = point // WIDE
-    lo = point - hi * WIDE
-    hi_mask = lax.broadcasted_iota(jnp.int32, (n_hi, n_obs), 0) == hi
-    lo_hot[...] = jnp.where(
-        lax.broadcasted_iota(jnp.int32, (WIDE, n_obs), 0) == lo, 1.0, 0.0
-    ).astype(BF16)
-    copies[1].wait()
-    copies[2].wait()
-    u = [jac_ref[a : a + 1, :] for a in range(3)]
-    v = [jac_ref[3 + a : 4 + a, :] for a in range(3)]
-    ru, rv = resid_ref[0:1, :], resid_ref[1:2, :]
-    terms = [u[a] * u[b] + v[a] * v[b] for a, b in ((0, 0), (0, 1), (0, 2), (1, 1), (1, 2), (2, 2))]
-    terms += [u[a] * ru + v[a] * rv for a in range(3)]
-    blocks = []
-    for part in zip(*[split_pair(t) for t in terms]):
-        blocks += [jnp.where(hi_mask, t, 0.0).astype(BF16) for t in part]
-    left = jnp.concatenate(blocks, axis=0)
-    both = lax.dot_general(
-        left, lo_hot[...], (((1,), (1,)), ((), ())), preferred_element_type=F32
-    )
-    local = both[: 9 * n_hi] + both[9 * n_hi :]
+    for copy in copies[:3]:
+        copy.wait()
+    local = jnp.zeros((9 * n_hi, WIDE), F32)
+    parts = [pl.ds(start, CHUNK) for start in range(0, n_obs, CHUNK)]
+    for part in parts:
+        point = point_ref[:, part]
+        hi = point // WIDE
+        hi_mask = lax.broadcasted_iota(jnp.int32, (n_hi, CHUNK), 0) == hi
+        hot = jnp.where(
+            lax.broadcasted_iota(jnp.int32, (WIDE, CHUNK), 0) == point - hi * WIDE, 1.0, 0.0
+        ).astype(BF16)
+        lo_hot[:, part] = hot
+        u = [jac_ref[a : a + 1, part] for a in range(3)]
+        v = [jac_ref[3 + a : 4 + a, part] for a in range(3)]
+        ru, rv = resid_ref[0:1, part], resid_ref[1:2, part]
+        pairs = ((0, 0), (0, 1), (0, 2), (1, 1), (1, 2), (2, 2))
+        terms = [u[a] * u[b] + v[a] * v[b] for a, b in pairs]
+        terms += [u[a] * ru + v[a] * rv for a in range(3)]
+        blocks = []
+        for values in zip(*[split_pair(t) for t in terms]):
+            blocks += [jnp.where(hi_mask, t, 0.0).astype(BF16) for t in values]
+        both = lax.dot_general(
+            jnp.concatenate(blocks, axis=0),
+            hot,
+            (((1,), (1,)), ((), ())),
+            preferred_element_type=F32,
+        )
+        local = local + (both[: 9 * n_hi] + both[9 * n_hi :])
     for k in range(9):
         for half in range(WIDE // LANES):
             piece = local[k * n_hi : (k + 1) * n_hi, half * LANES : (half + 1) * LANES]
@@ -177,15 +183,14 @@
 
     copies[3].wait()
     copies[4].wait()
-    row_slot = slot_ref[...]
     eye = lax.broadcasted_iota(jnp.int32, (groups, groups), 0) == lax.broadcasted_iota(
         jnp.int32, (groups, groups), 1
     )
     slot_column = jnp.sum(
-        jnp.where(eye, row_slot.astype(F32), 0.0), axis=1, keepdims=True
+        jnp.where(eye, slot_ref[...].astype(F32), 0.0), axis=1, keepdims=True
     )
     group_iota = lax.broadcasted_iota(jnp.int32, (groups, n_obs), 0)
-    slots = jnp.sum(
+    slot_row[...] = jnp.sum(
         jnp.where(group_iota == cam_ref[...], slot_column, 0.0), axis=0, keepdims=True
     ).astype(jnp.int32)
 
@@ -213,20 +218,25 @@
     pieces = []
     for part in zip(*[split_pair(t) for t in picked]):
         pieces += [t.astype(BF16) for t in part]
-    found = jnp.dot(jnp.concatenate(pieces, axis=0), lo_hot[...], preferred_element_type=F32)
-    step_obs = []
-    for a in range(3):
-        both_parts = found[a * n_hi : (a + 1) * n_hi] + found[(3 + a) * n_hi : (4 + a) * n_hi]
-        step_obs.append(jnp.sum(jnp.where(hi_mask, both_parts, 0.0), axis=0, keepdims=True))
-    cu = ru + u[0] * step_obs[0] + u[1] * step_obs[1] + u[2] * step_obs[2]
-    cv = rv + v[0] * step_obs[0] + v[1] * step_obs[1] + v[2] * step_obs[2]
-    member = group_iota == slots
-    weights = jnp.concatenate(
-        [jnp.where(member, cu, 0.0).astype(BF16), jnp.where(member, cv, 0.0).astype(BF16)], axis=0
-    )
+    table_rows = jnp.concatenate(pieces, axis=0)
     copies[5].wait()
-    product = jnp.dot(weights, cam_vmem[...], preferred_element_type=F32)
-    partial = product[:groups, :CAMP] + product[groups:, CAMP:]
+    partial = jnp.zeros((groups, CAMP), F32)
+    group_iota = lax.broadcasted_iota(jnp.int32, (groups, CHUNK), 0)
+    for part in parts:
+        found = jnp.dot(table_rows, lo_hot[:, part], preferred_element_type=F32)
+        hi_mask = lax.broadcasted_iota(jnp.int32, (n_hi, CHUNK), 0) == point_ref[:, part] // WIDE
+        cu, cv = resid_ref[0:1, part], resid_ref[1:2, part]
+        for a in range(3):
+            pair = found[a * n_hi : (a + 1) * n_hi] + found[(3 + a) * n_hi : (4 + a) * n_hi]
+            step = jnp.sum(jnp.where(hi_mask, pair, 0.0), axis=0, keepdims=True)
+            cu = cu + jac_ref[a : a + 1, part] * step
+            cv = cv + jac_ref[3 + a : 4 + a, part] * step
+        member = group_iota == slot_row[:, part]
+        weights = jnp.concatenate(
+            [jnp.where(member, c, 0.0).astype(BF16) for c in (cu, cv)], axis=0
+        )
+        product = jnp.dot(weights, cam_vmem[part, :], preferred_element_type=F32)
+        partial = partial + (product[:groups, :CAMP] + product[groups:, CAMP:])
     part_send[...] = partial.reshape(n_dev, gpd, CAMP)
 
     every_peer(
@@ -271,14 +281,21 @@
     grad_out.wait()
 
 
-def write_out(step_in, grad_in, step_hbm, grad_hbm, sems):
-    copies = [
-        pltpu.make_async_copy(step_in, step_hbm, sems.at[0]),
-        pltpu.make_async_copy(grad_in, grad_hbm, sems.at[1]),
+def write_out(step_in, grad_in, step_hbm, grad_hbm, step_held, grad_held, sems):
+    arrive = [
+        pltpu.make_async_copy(grad_in, grad_held, sems.at[0]),
+        pltpu.make_async_copy(step_in, step_held, sems.at[1]),
     ]
-    for copy in copies:
+    leave = [
+        pltpu.make_async_copy(grad_held, grad_hbm, sems.at[2]),
+        pltpu.make_async_copy(step_held, step_hbm, sems.at[3]),
+    ]
+    for copy in arrive:
         copy.start()
-    for copy in copies:
+    for first, second in zip(arrive, leave):
+        first.wait()
+        second.start()
+    for copy in leave:
         copy.wait()
 
 
@@ -313,6 +330,7 @@
                 pltpu.VMEM((1, n_obs), jnp.int32),
                 pltpu.VMEM((1, n_obs), jnp.int32),
                 pltpu.VMEM((1, groups), jnp.int32),
+                pltpu.VMEM((1, n_obs), jnp.int32),
                 pltpu.VMEM((n_obs, 2 * CAMP), BF16),
                 pltpu.VMEM((WIDE, n_obs), BF16),
                 pltpu.VMEM((n_own, 9, per_row, LANES), F32),
@@ -342,7 +360,11 @@
             out_shape=shapes,
             in_specs=[hbm, hbm],
             out_specs=(hbm, hbm),
-            scratch_shapes=[pltpu.SemaphoreType.DMA((2,))],
+            scratch_shapes=[
+                pltpu.VMEM((3, points), F32),
+                pltpu.VMEM((gpd, CAMP), F32),
+                pltpu.SemaphoreType.DMA((4,)),
+            ],
             compiler_params=pltpu.CompilerParams(vmem_limit_bytes=VMEM_BYTES),
         )(*results)
 

time: 26.6 us -> 25.4 us (0.955)
  Pallas kernels: 25.1 us -> 23.8 us
    pallas_call x1, Pallas kernels: 3.14 us -> 1.51 us  [per_device(): pl.pallas_call(write_out, out_shape=shapes, in_specs=[hbm, hbm], out_spec...]
    pallas_call x1, Pallas kernels: 22 us -> 22.3 us  [per_device(): pl.pallas_call(functools.partial(kernel, n_img, n_lm, n_own, groups), out...]
where the time goes in v3:
time: 25.4 us; the launch traced here: 25.1 us
  Pallas kernels  23.8 us (94%)
  between operations  1.29 us (5%)
    pallas_call x1, Pallas kernels, per_device(): pl.pallas_call(functools.partial(kernel, n_img, n_lm, n_own, groups), out...  22.3 us
    pallas_call x1, Pallas kernels, per_device(): pl.pallas_call(write_out, out_shape=shapes, in_specs=[hbm, hbm], out_spec...  1.51 us

profile of v3, /device:TPU:0, one launch (start us, length us, event | category | flops | bytes accessed | tf_op | source)
XLA Modules:
  0.0 25.1 jit_solution(9061910452854889455)
XLA Ops:
  1.3 22.3 %shard_map.86 = (f32[3,4096]{1,0:T(4,128)}, f32[2,128]{1,0:T(2,128)}) custom-call(f32[1]{0:T(128)S(6)} %copy.9.damping_ref, f32[6,2048]{1,0:T(8,128)} %jac_hbm.1, f32[2,2048]{1,0:T(2,128)} %resid_hbm.1, s32[1,2048]{1,0:T(1,128)} %bitcast.3, s32[1,2048]{1,0:T(1,128)} %bitcast.4, s32[1,64]{1,0:T(1,128)} %bitcast.5, bf16[2048,256]{1,0:T(8,128)(2,1)} %jac_cam_hbm.1), custom_call_target="tpu_custom_call" | custom-call | tf_op jit(solution)/shard_map/pallas_call | solution.py:319
  23.6 1.5 %shard_map.87 = (f32[3,4096]{1,0:T(4,128)}, f32[2,128]{1,0:T(2,128)}) custom-call(f32[3,4096]{1,0:T(4,128)} %get-tuple-element.4.step_in, f32[2,128]{1,0:T(2,128)} %get-tuple-element.5.grad_in), custom_call_target="tpu_custom_call" | custom-call | tf_op jit(solution)/shard_map/pallas_call | solution.py:358

commit v4 on v2

--- a/solution.py
+++ b/solution.py
@@ -271,14 +271,21 @@
     grad_out.wait()
 
 
-def write_out(step_in, grad_in, step_hbm, grad_hbm, sems):
-    copies = [
-        pltpu.make_async_copy(step_in, step_hbm, sems.at[0]),
-        pltpu.make_async_copy(grad_in, grad_hbm, sems.at[1]),
+def write_out(step_in, grad_in, step_hbm, grad_hbm, step_held, grad_held, sems):
+    arrive = [
+        pltpu.make_async_copy(grad_in, grad_held, sems.at[0]),
+        pltpu.make_async_copy(step_in, step_held, sems.at[1]),
     ]
-    for copy in copies:
+    leave = [
+        pltpu.make_async_copy(grad_held, grad_hbm, sems.at[2]),
+        pltpu.make_async_copy(step_held, step_hbm, sems.at[3]),
+    ]
+    for copy in arrive:
         copy.start()
-    for copy in copies:
+    for first, second in zip(arrive, leave):
+        first.wait()
+        second.start()
+    for copy in leave:
         copy.wait()
 
 
@@ -342,7 +349,11 @@
             out_shape=shapes,
             in_specs=[hbm, hbm],
             out_specs=(hbm, hbm),
-            scratch_shapes=[pltpu.SemaphoreType.DMA((2,))],
+            scratch_shapes=[
+                pltpu.VMEM((3, points), F32),
+                pltpu.VMEM((gpd, CAMP), F32),
+                pltpu.SemaphoreType.DMA((4,)),
+            ],
             compiler_params=pltpu.CompilerParams(vmem_limit_bytes=VMEM_BYTES),
         )(*results)
 

time: 26.6 us -> 25 us (0.940)
  Pallas kernels: 25.1 us -> 23.5 us
    pallas_call x1, Pallas kernels: 3.14 us -> 1.51 us  [per_device(): pl.pallas_call(write_out, out_shape=shapes, in_specs=[hbm, hbm], out_spec...]
where the time goes in v4:
time: 25 us; the launch traced here: 24.8 us
  Pallas kernels  23.5 us (94%)
  between operations  1.29 us (5%)
    pallas_call x1, Pallas kernels, per_device(): pl.pallas_call(functools.partial(kernel, n_img, n_lm, n_own, groups), out...  22 us
    pallas_call x1, Pallas kernels, per_device(): pl.pallas_call(write_out, out_shape=shapes, in_specs=[hbm, hbm], out_spec...  1.51 us

profile of v4, /device:TPU:0, one launch (start us, length us, event | category | flops | bytes accessed | tf_op | source)
XLA Modules:
  0.0 24.8 jit_solution(12605049342813690462)
XLA Ops:
  1.3 22.0 %shard_map.86 = (f32[3,4096]{1,0:T(4,128)}, f32[2,128]{1,0:T(2,128)}) custom-call(f32[1]{0:T(128)S(6)} %copy.9.damping_ref, f32[6,2048]{1,0:T(8,128)} %jac_hbm.1, f32[2,2048]{1,0:T(2,128)} %resid_hbm.1, s32[1,2048]{1,0:T(1,128)} %bitcast.3, s32[1,2048]{1,0:T(1,128)} %bitcast.4, s32[1,64]{1,0:T(1,128)} %bitcast.5, bf16[2048,256]{1,0:T(8,128)(2,1)} %jac_cam_hbm.1), custom_call_target="tpu_custom_call" | custom-call | tf_op jit(solution)/shard_map/pallas_call | solution.py:309
  23.2 1.5 %shard_map.87 = (f32[3,4096]{1,0:T(4,128)}, f32[2,128]{1,0:T(2,128)}) custom-call(f32[3,4096]{1,0:T(4,128)} %get-tuple-element.4.step_in, f32[2,128]{1,0:T(2,128)} %get-tuple-element.5.grad_in), custom_call_target="tpu_custom_call" | custom-call | tf_op jit(solution)/shard_map/pallas_call | solution.py:347

commit v5 on v4

--- a/solution.py
+++ b/solution.py
@@ -105,8 +105,8 @@
 
     copies[0].wait()
     point = point_ref[...]
-    hi = point // WIDE
-    lo = point - hi * WIDE
+    hi = lax.shift_right_logical(point, WIDE.bit_length() - 1)
+    lo = lax.bitwise_and(point, WIDE - 1)
     hi_mask = lax.broadcasted_iota(jnp.int32, (n_hi, n_obs), 0) == hi
     lo_hot[...] = jnp.where(
         lax.broadcasted_iota(jnp.int32, (WIDE, n_obs), 0) == lo, 1.0, 0.0

time: 25 us -> 25 us (level)
  no operation moved by 1% of the time
where the time goes in v5:
time: 25 us; the launch traced here: 24.8 us
  Pallas kernels  23.5 us (94%)
  between operations  1.29 us (5%)
    pallas_call x1, Pallas kernels, per_device(): pl.pallas_call(functools.partial(kernel, n_img, n_lm, n_own, groups), out...  22 us
    pallas_call x1, Pallas kernels, per_device(): pl.pallas_call(write_out, out_shape=shapes, in_specs=[hbm, hbm], out_spec...  1.51 us

profile of v5, /device:TPU:0, one launch (start us, length us, event | category | flops | bytes accessed | tf_op | source)
XLA Modules:
  0.0 24.8 jit_solution(12451701554909857196)
XLA Ops:
  1.3 22.0 %shard_map.86 = (f32[3,4096]{1,0:T(4,128)}, f32[2,128]{1,0:T(2,128)}) custom-call(f32[1]{0:T(128)S(6)} %copy.9.damping_ref, f32[6,2048]{1,0:T(8,128)} %jac_hbm.1, f32[2,2048]{1,0:T(2,128)} %resid_hbm.1, s32[1,2048]{1,0:T(1,128)} %bitcast.3, s32[1,2048]{1,0:T(1,128)} %bitcast.4, s32[1,64]{1,0:T(1,128)} %bitcast.5, bf16[2048,256]{1,0:T(8,128)(2,1)} %jac_cam_hbm.1), custom_call_target="tpu_custom_call" | custom-call | tf_op jit(solution)/shard_map/pallas_call | solution.py:309
  23.3 1.5 %shard_map.87 = (f32[3,4096]{1,0:T(4,128)}, f32[2,128]{1,0:T(2,128)}) custom-call(f32[3,4096]{1,0:T(4,128)} %get-tuple-element.4.step_in, f32[2,128]{1,0:T(2,128)} %get-tuple-element.5.grad_in), custom_call_target="tpu_custom_call" | custom-call | tf_op jit(solution)/shard_map/pallas_call | solution.py:347
